TPU v7x, 32 devices: a whole 2x2x4 slice. The times are simulated.
32 devices in a mesh: groups: 2 (over y), feat: 4 (over z), layer: 4 (over x, core).
Axes of the slice: x: 2, y: 2, z: 4, core: 2. Of those that a mesh axis runs over, the one named last changes fastest.
Arguments:
- inputs: bfloat16 [2, 1024, 2048], P(None, ('groups', 'feat')), parts along dimension 1, may hold values from -6 to 6
- targets: bfloat16 [1024, 2, 2048], P(('groups', 'feat')), parts along dimension 0, may hold values from -6 to 6
- block_mask: int32 [2, 256, 1024], P(None, 'feat', 'groups'), parts along dimension 2, may hold values 0 or 1
- enc_weight: bfloat16 [2, 32768, 2048], P(None, ('feat', 'layer')), may hold values from -0.125 to 0.125
- enc_bias: float32 [2, 32768], P(None, ('feat', 'layer')), may hold values from -3 to 3
- threshold: float32 [2, 32768], P(None, ('feat', 'layer')), may hold values from 0.3 to 1.2
- dec_weight: bfloat16 [3, 32768, 2048], P(None, ('feat', 'layer')), may hold values from -0.09375 to 0.09375
Outputs:
- grad_enc: bfloat16 [4, 32768, 2048], P('groups', ('feat', 'layer')), parts along dimension 0
- grad_bias: float32 [4, 32768], P('groups', ('feat', 'layer')), parts along dimension 0
- grad_threshold: float32 [4, 32768], P('groups', ('feat', 'layer')), parts along dimension 0
- grad_dec: bfloat16 [6, 32768, 2048], P('groups', ('feat', 'layer')), parts along dimension 0
There are 2 independent parts, one for each index of `groups`. A program takes and returns all parts, laid end to end along the dimension named above; an argument that names none is the same for every part. Nothing has to cross between parts.
All inputs are finite; a program needn't handle non-finite values. No bound on the sum of `block_mask` on one device may be relied on, other than what follows from the above.
Results may differ from a plain program's by a relative error of at most 0.015.
Values may be sent and summed in bfloat16 or wider, within the bound.
A program may use at most 256 MiB of HBM per device.

v0:
```python
import jax
import jax.numpy as jnp
from jax import lax
from jax.sharding import PartitionSpec as P

BLOCK = 128


BAND = 0.2


def per_device(inputs, targets, block_mask, enc_weight, enc_bias, threshold, dec_weight):
    layer_count = enc_weight.shape[0]
    feat_width = enc_weight.shape[1]
    model_width = enc_weight.shape[2]
    local_rows = inputs.shape[1]
    layer_place = lax.axis_index("layer")
    pairs = [
        (source, target) for source in range(layer_count) for target in range(source, layer_count)
    ]
    whole = lax.all_gather(inputs, "feat", axis=1, tiled=True)
    preact = (
        jnp.einsum("lrd,lfd->lrf", whole, enc_weight, preferred_element_type=jnp.float32)
        + enc_bias[:, None, :]
    )
    block_count = block_mask.shape[1]
    positions = layer_place * feat_width + jnp.arange(feat_width, dtype=jnp.int32)
    select = (
        positions[:, None] // BLOCK == jnp.arange(block_count, dtype=jnp.int32)[None, :]
    ).astype(jnp.float32)
    gates = jnp.einsum("lbr,kb->lrk", block_mask.astype(jnp.float32), select)
    squash = jax.nn.sigmoid((preact - threshold[:, None, :]) / BAND)
    hidden = (gates * preact * squash).astype(jnp.bfloat16)
    columns = []
    for target in range(layer_count):
        total = jnp.zeros((local_rows * lax.axis_size("feat"), model_width), jnp.float32)
        for index, (source, goal) in enumerate(pairs):
            if goal == target:
                part_rows = hidden[source]
                total = total + jnp.dot(
                    part_rows, dec_weight[index], preferred_element_type=jnp.float32
                )
        columns.append(total)
    decoded = lax.psum_scatter(
        jnp.stack(columns, 1).astype(jnp.bfloat16), "feat", scatter_dimension=0, tiled=True
    )
    own_sum = lax.psum(decoded, "layer").astype(jnp.float32)
    error = (own_sum - targets.astype(jnp.float32)).astype(jnp.bfloat16)
    pieces = lax.all_gather(error, "feat", axis=0, tiled=True)
    count = pieces.shape[0]
    back_parts = [jnp.zeros((count, feat_width), jnp.float32) for source in range(layer_count)]
    new_grads = []
    for index, (source, goal) in enumerate(pairs):
        part_rows = hidden[source]
        new_grads.append(
            lax.dot_general(
                part_rows,
                pieces[:, goal],
                (((0,), (0,)), ((), ())),
                preferred_element_type=jnp.float32,
            )
        )
        back_parts[source] = back_parts[source] + lax.dot_general(
            pieces[:, goal],
            dec_weight[index],
            (((1,), (1,)), ((), ())),
            preferred_element_type=jnp.float32,
        )
    stacked = jnp.stack(back_parts, 0)
    back_grad = stacked
    dec_sum, back_grad = (jnp.stack(new_grads, 0), back_grad)
    bend = squash * (1.0 - squash) / BAND
    slope = gates * (squash + preact * bend)
    grad_pre = back_grad * slope
    grad_bias = jnp.sum(grad_pre, axis=1)
    grad_threshold = -jnp.sum(back_grad * gates * preact * bend, axis=1)
    grad_rounded = grad_pre.astype(jnp.bfloat16)
    grad_enc = jnp.einsum(
        "lrf,lrd->lfd", grad_rounded, whole, preferred_element_type=jnp.float32
    ).astype(jnp.bfloat16)
    return (grad_enc, grad_bias, grad_threshold, dec_sum.astype(jnp.bfloat16))


def solution(mesh):
    return jax.shard_map(
        per_device,
        mesh=mesh,
        in_specs=(
            P(None, ("groups", "feat"), None),
            P(("groups", "feat"), None, None),
            P(None, "feat", "groups"),
            P(None, ("feat", "layer"), None),
            P(None, ("feat", "layer")),
            P(None, ("feat", "layer")),
            P(None, ("feat", "layer"), None),
        ),
        out_specs=(
            P("groups", ("feat", "layer"), None),
            P("groups", ("feat", "layer")),
            P("groups", ("feat", "layer")),
            P("groups", ("feat", "layer"), None),
        ),
        check_vma=False,
    )
```

profile of v0, /device:TPU:0, one launch (start us, length us, event | category | flops | bytes accessed | tf_op | source)
XLA Modules:
  0.0 442.6 jit_solution(11396535841463564126)
XLA Ops:
  7.2 0.0 all-gather.3.cloned.1.call-start
  7.2 0.7 all-gather.3.cloned.1.call-update
  7.9 0.0 reduce-scatter.2.cloned.1.call-start
  8.0 0.0 copy-start.2
  8.0 0.0 copy-start.3
  8.0 0.0 copy-start.6
  8.0 85.1 %all-gather.3.cloned.1.call-done = bf16[2,512,2048]{2,1,0:T(8,128)(2,1)} async-done(((bf16[2,128,2048]{2,1,0:T(8,128)(2,1)}), bf16[2,512,2048]{2,1,0:T(8,128)(2,1)}) %all-gather.3.cloned.1.call-update) | async-done | bytes 4194320 | tf_op jit(solution)/shard_map/all_gather | solution.py:21
  93.1 15.7 %fusion.52 = f32[2,512,2048]{2,1,0:T(8,128)} fusion(bf16[2,512,2048]{2,1,0:T(8,128)(2,1)} %all-gather.3.cloned.1.call-done, bf16[2,2048,2048]{2,1,0:T(8,128)(2,1)} %param.10), kind=kOutput, calls=%fused_computation.64 | convolution fusion | flops 8589934592 | bytes 29360128 | tf_op jit(solution)/shard_map/lrd,lfd->lrf/dot_general | solution.py:23
  108.8 0.0 copy-done.2
  108.8 0.0 copy-done.3
  108.8 0.0 copy-done.6
  108.8 7.1 %fusion.14 = (bf16[2,512,2048]{2,1,0:T(8,128)(2,1)S(1)}, f32[2048,2,512]{0,2,1:T(8,128)}) fusion(f32[2,512,2048]{2,1,0:T(8,128)} %fusion.52, f32[2,2048]{1,0:T(2,128)S(1)} %copy-done.2, f32[2,2048]{1,0:T(2,128)S(1)} %copy-done.3, s32[2,64,512]{2,1,0:T(8,128)S(1)} %copy-done.6, s32[2048]{0:T(1024)S(1)} %add_select_fusion), kind=kOutput, calls=%fused_computation.21 | convolution fusion | flops 287506432 | bytes 21274624 | tf_op jit(solution)/shard_map/lbr,kb->lrk/dot_general | solution.py:31
  115.9 0.0 copy-start.7
  115.9 9.6 %fusion.36 = bf16[512,1,2048]{2,0,1:T(8,128)(2,1)S(1)} fusion(bf16[3,2048,2048]{2,1,0:T(8,128)(2,1)} %param.13, bf16[2,512,2048]{2,1,0:T(8,128)(2,1)S(1)} %get-tuple-element.7), kind=kOutput, calls=%fused_computation.42 | convolution fusion | flops 4296015872 | bytes 12582912 | tf_op jit(solution)/shard_map/dot_general | solution.py:40
  125.5 6.9 %fusion.3 = f32[512,2048]{1,0:T(8,128)S(1)} fusion(bf16[3,2048,2048]{2,1,0:T(8,128)(2,1)} %param.13, bf16[2,512,2048]{2,1,0:T(8,128)(2,1)S(1)} %get-tuple-element.7), kind=kOutput, calls=%fused_computation.7 | convolution fusion | flops 4294967296 | bytes 14680064 | tf_op jit(solution)/shard_map/dot_general | solution.py:40
  132.4 0.0 copy-done.7
  132.4 8.1 %fusion.39 = bf16[512,1,2048]{2,0,1:T(8,128)(2,1)S(1)} fusion(f32[512,2048]{1,0:T(8,128)S(1)} %fusion.3, bf16[3,2048,2048]{2,1,0:T(8,128)(2,1)} %param.13, bf16[2,512,2048]{2,1,0:T(8,128)(2,1)S(1)} %get-tuple-element.7), kind=kOutput, calls=%fused_computation.43 | convolution fusion | flops 4297064448 | bytes 16777216 | tf_op jit(solution)/shard_map/dot_general | solution.py:40
  140.5 0.0 copy-start.1
  140.5 2.3 pad_maximum_fusion.2
  142.8 0.0 reduce-scatter.2.cloned.1.call-update
  142.9 0.0 all-reduce.2.cloned.1.call-start
  142.9 75.4 %reduce-scatter.2.cloned.1.call-done = bf16[128,2,2048]{2,0,1:T(8,128)(2,1)} async-done(((bf16[512,2,2048]{2,0,1:T(8,128)(2,1)}), bf16[128,2,2048]{2,0,1:T(8,128)(2,1)}) %reduce-scatter.2.cloned.1.call-update) | async-done | bytes 1048592 | tf_op jit(solution)/shard_map/reduce_scatter | solution.py:44
  218.3 0.0 all-reduce.2.cloned.1.call-update
  218.3 0.2 all-gather.5.cloned.1.call-start
  218.5 38.9 %all-reduce.2.cloned.1.call-done = bf16[128,2,2048]{2,0,1:T(8,128)(2,1)} async-done(((bf16[128,2,2048]{2,0,1:T(8,128)(2,1)}), bf16[128,2,2048]{2,0,1:T(8,128)(2,1)}) %all-reduce.2.cloned.1.call-update) | async-done | bytes 1048592 | tf_op jit(solution)/shard_map/psum | solution.py:47
  257.5 0.0 copy-done.1
  257.5 2.8 subtract_convert_fusion
  260.3 0.0 all-gather.5.cloned.1.call-update
  260.3 81.3 %all-gather.5.cloned.1.call-done = bf16[512,2,2048]{2,0,1:T(8,128)(2,1)} async-done(((bf16[128,2,2048]{2,0,1:T(8,128)(2,1)}), bf16[512,2,2048]{2,0,1:T(8,128)(2,1)}) %all-gather.5.cloned.1.call-update) | async-done | bytes 4194320 | tf_op jit(solution)/shard_map/all_gather | solution.py:49
  341.6 0.0 copy-start.4
  341.6 10.6 %fusion.26 = f32[1,512,2048]{2,1,0:T(8,128)} fusion(bf16[3,2048,2048]{2,1,0:T(8,128)(2,1)} %param.13, bf16[512,2,2048]{2,0,1:T(8,128)(2,1)} %all-gather.5.cloned.1.call-done), kind=kOutput, calls=%fused_computation.40 | convolution fusion | flops 4294967296 | bytes 14680064 | tf_op jit(solution)/shard_map/dot_general | solution.py:63
  352.2 0.0 copy-done.4
  352.2 0.0 slice-start
  352.2 9.6 %fusion.5 = f32[512,2048]{1,0:T(8,128)} fusion(bf16[3,2048,2048]{2,1,0:T(8,128)(2,1)} %param.13, bf16[512,2,2048]{2,0,1:T(8,128)(2,1)S(1)} %copy-done.4), kind=kOutput, calls=%fused_computation.9 | convolution fusion | flops 4294967296 | bytes 14680064 | tf_op jit(solution)/shard_map/dot_general | solution.py:63
  361.9 11.8 %add_bitcast_fusion = f32[1,512,2048]{2,1,0:T(8,128)} fusion(f32[512,2048]{1,0:T(8,128)} %fusion.5, bf16[3,2048,2048]{2,1,0:T(8,128)(2,1)} %param.13, bf16[512,2,2048]{2,0,1:T(8,128)(2,1)} %all-gather.5.cloned.1.call-done), kind=kOutput, calls=%fused_computation.38 | convolution fusion | flops 4296015872 | bytes 18874368 | tf_op jit(solution)/shard_map/dot_general | solution.py:63
  373.7 0.0 slice-done
  373.7 0.0 slice-done.2
  373.7 0.0 slice-done.1
  373.7 0.0 slice-done.3
  373.7 9.9 %fusion.50 = (f32[2,2048]{1,0:T(2,128)}, bf16[2,512,2048]{2,1,0:T(8,128)(2,1)}, f32[2,2048]{1,0:T(2,128)S(1)}) fusion(f32[2,2048]{1,0:T(2,128)S(1)} %copy-done.2, f32[2,512,2048]{2,1,0:T(8,128)S(1)} %bitcast.88, f32[2,2048]{1,0:T(2,128)S(1)} %copy-done.3, f32[2048,2,512]{0,2,1:T(8,128)S(1)} %bitcast.90, f32[1,512,2048]{2,1,0:T(8,128)} %fusion.26, ...), kind=kLoop, calls=%fused_computation.63 | loop fusion | flops 41934848 | bytes 29425664 | tf_op jit(solution)/shard_map/reduce_sum | solution.py:75
  383.6 0.6 neg.7
  384.2 6.9 %convert_bitcast_fusion.1 = bf16[1,2048,2048]{2,1,0:T(8,128)(2,1)S(1)} fusion(bf16[2,512,2048]{2,1,0:T(8,128)(2,1)} %copy-done.7, bf16[512,2,2048]{2,0,1:T(8,128)(2,1)} %all-gather.5.cloned.1.call-done), kind=kOutput, calls=%fused_computation.27 | convolution fusion | flops 4299161600 | bytes 12582912 | tf_op jit(solution)/shard_map/dot_general | solution.py:56
  391.1 0.0 copy-done.5
  391.2 6.4 %convert_bitcast_fusion = bf16[1,2048,2048]{2,1,0:T(8,128)(2,1)S(1)} fusion(bf16[2,512,2048]{2,1,0:T(8,128)(2,1)} %copy-done.7, bf16[512,2,2048]{2,0,1:T(8,128)(2,1)S(1)} %copy-done.5), kind=kOutput, calls=%fused_computation.26 | convolution fusion | flops 4299161600 | bytes 12582912 | tf_op jit(solution)/shard_map/dot_general | solution.py:56
  397.6 8.4 %convert_bitcast_fusion.2 = bf16[1,2048,2048]{2,1,0:T(8,128)(2,1)} fusion(bf16[512,2,2048]{2,0,1:T(8,128)(2,1)S(1)} %copy-done.5, bf16[2,512,2048]{2,1,0:T(8,128)(2,1)} %copy-done.7), kind=kOutput, calls=%fused_computation.28 | convolution fusion | flops 4299161600 | bytes 12582912 | tf_op jit(solution)/shard_map/dot_general | solution.py:56
  406.1 14.5 %pad_maximum_fusion = bf16[3,2048,2048]{2,1,0:T(8,128)(2,1)} fusion(bf16[1,2048,2048]{2,1,0:T(8,128)(2,1)S(1)} %convert_bitcast_fusion, bf16[1,2048,2048]{2,1,0:T(8,128)(2,1)S(1)} %convert_bitcast_fusion.1, bf16[1,2048,2048]{2,1,0:T(8,128)(2,1)} %convert_bitcast_fusion.2), kind=kLoop, calls=%fused_computation | loop fusion | flops 25165824 | bytes 50331648 | tf_op jit(solution)/shard_map/stack | solution.py:71
  420.6 0.0 copy-done
  420.6 15.0 %convolution_convert_fusion = bf16[2,2048,2048]{2,1,0:T(8,128)(2,1)} fusion(bf16[2,512,2048]{2,1,0:T(8,128)(2,1)} %all-gather.3.cloned.1.call-done, bf16[2,512,2048]{2,1,0:T(8,128)(2,1)S(1)} %copy-done), kind=kOutput, calls=%fused_computation.2 | convolution fusion | flops 8598323200 | bytes 25165824 | tf_op jit(solution)/shard_map/lrf,lrd->lfd/dot_general | solution.py:78
  (8 shorter events, 0.0 us)
Async XLA Ops:
  7.2 85.9 %all-gather.3.cloned.1.call-start = ((), (), s32[]{:S(2)}) async-start(), calls=%async_computation.1 | async-start | bytes 5242880 | tf_op jit(solution)/shard_map/all_gather | solution.py:21
  7.9 210.4 %reduce-scatter.2.cloned.1.call-start = ((), (), s32[]{:S(2)}) async-start(), calls=%async_computation.2 | async-start | bytes 5242880 | tf_op jit(solution)/shard_map/reduce_scatter | solution.py:44
  8.0 100.8 %copy-start.2 = (f32[2,2048]{1,0:T(2,128)S(1)}, f32[2,2048]{1,0:T(2,128)}, u32[]{:S(2)}) copy-start(f32[2,2048]{1,0:T(2,128)} %param.12) | copy-start | bytes 49156
  8.0 100.8 %copy-start.3 = (f32[2,2048]{1,0:T(2,128)S(1)}, f32[2,2048]{1,0:T(2,128)}, u32[]{:S(2)}) copy-start(f32[2,2048]{1,0:T(2,128)} %param.11) | copy-start | bytes 49156
  8.0 100.8 %copy-start.6 = (s32[2,64,512]{2,1,0:T(8,128)S(1)}, s32[2,64,512]{2,1,0:T(8,128)}, u32[]{:S(2)}) copy-start(s32[2,64,512]{2,1,0:T(8,128)} %param.9) | copy-start | bytes 786436
  115.9 16.5 %copy-start.7 = (bf16[2,512,2048]{2,1,0:T(8,128)(2,1)}, bf16[2,512,2048]{2,1,0:T(8,128)(2,1)S(1)}, u32[]{:S(2)}) copy-start(bf16[2,512,2048]{2,1,0:T(8,128)(2,1)S(1)} %get-tuple-element.7) | copy-start | bytes 12582916
  140.5 117.0 %copy-start.1 = (bf16[128,2,2048]{2,1,0:T(2,128)(2,1)S(1)}, bf16[128,2,2048]{2,1,0:T(2,128)(2,1)}, u32[]{:S(2)}) copy-start(bf16[128,2,2048]{2,1,0:T(2,128)(2,1)} %param.8) | copy-start | bytes 3145732
  142.9 114.6 %all-reduce.2.cloned.1.call-start = ((), (), s32[]{:S(2)}) async-start(), calls=%async_computation.3 | async-start | bytes 2097152 | tf_op jit(solution)/shard_map/psum | solution.py:47
  218.3 123.3 %all-gather.5.cloned.1.call-start = ((), (), s32[]{:S(2)}) async-start(), calls=%async_computation.4 | async-start | bytes 5242880 | tf_op jit(solution)/shard_map/all_gather | solution.py:49
  341.6 10.6 %copy-start.4 = (bf16[512,2,2048]{2,0,1:T(8,128)(2,1)S(1)}, bf16[512,2,2048]{2,0,1:T(8,128)(2,1)}, u32[]{:S(2)}) copy-start(bf16[512,2,2048]{2,0,1:T(8,128)(2,1)} %all-gather.5.cloned.1.call-done) | copy-start | bytes 12582916
  352.2 21.5 %slice-start = ((s8[8388608]{0:T(1024)(128)(4,1)}), s8[4194304]{0:T(1024)(128)(4,1)S(1)}, s32[]{:S(2)}) async-start(s8[8388608]{0:T(1024)(128)(4,1)} %bitcast.87), calls=%async_computation.5 | async-start | bytes 8388608
  352.2 21.5 %slice-start.2 = ((s8[8388608]{0:T(1024)(128)(4,1)}), s8[4194304]{0:T(1024)(128)(4,1)S(1)}, s32[]{:S(2)}) async-start(s8[8388608]{0:T(1024)(128)(4,1)} %bitcast.89), calls=%async_computation.7 | async-start | bytes 8388608
  361.9 11.8 %slice-start.1 = ((s8[8388608]{0:T(1024)(128)(4,1)}), s8[4194304]{0:T(1024)(128)(4,1)S(1)}, s32[]{:S(2)}) async-start(s8[8388608]{0:T(1024)(128)(4,1)} %bitcast.87), calls=%async_computation.6 | async-start | bytes 8388608
  361.9 11.8 %slice-start.3 = ((s8[8388608]{0:T(1024)(128)(4,1)}), s8[4194304]{0:T(1024)(128)(4,1)S(1)}, s32[]{:S(2)}) async-start(s8[8388608]{0:T(1024)(128)(4,1)} %bitcast.89), calls=%async_computation.8 | async-start | bytes 8388608
  384.2 6.9 %copy-start.5 = (bf16[512,2,2048]{2,0,1:T(8,128)(2,1)S(1)}, bf16[512,2,2048]{2,0,1:T(8,128)(2,1)}, u32[]{:S(2)}) copy-start(bf16[512,2,2048]{2,0,1:T(8,128)(2,1)} %all-gather.5.cloned.1.call-done) | copy-start | bytes 12582916
  406.1 14.5 %copy-start = (bf16[2,512,2048]{2,1,0:T(8,128)(2,1)S(1)}, bf16[2,512,2048]{2,1,0:T(8,128)(2,1)}, u32[]{:S(2)}) copy-start(bf16[2,512,2048]{2,1,0:T(8,128)(2,1)} %get-tuple-element.5) | copy-start | bytes 12582916
Sparse Core Ops, SparseCore 0:
  9.6 83.4 all-gather.2
  143.0 75.2 reduce-scatter.1
  220.8 36.6 all-reduce.1
  260.4 81.1 all-gather.4
where the time goes:
time: 451 us; the launch traced here: 443 us
  waiting for transfers between devices  281 us (62%)
  matrix products  116 us (26%)
  other arithmetic  30.1 us (7%)
  between operations  14.3 us (3%)
    all_gather x1, waiting for transfers between devices, per_device(): whole = lax.all_gather(inputs, 'feat', axis=1, tiled=True)  85.1 us
    all_gather x1, waiting for transfers between devices, per_device(): pieces = lax.all_gather(error, 'feat', axis=0, tiled=True)  81.3 us
    reduce_scatter x1, waiting for transfers between devices, per_device(): lax.psum_scatter(jnp.stack(columns, 1).astype(jnp.bfloat16), 'feat', scat...  75.4 us
    psum x1, waiting for transfers between devices, per_device(): own_sum = lax.psum(decoded, 'layer').astype(jnp.float32)  38.9 us
    dot_general x3, matrix products, per_device(): lax.dot_general(pieces[:, goal], dec_weight[index], (((1,), (1,)), ((), (...  32.1 us
    dot_general x3, matrix products, per_device(): jnp.dot(part_rows, dec_weight[index], preferred_element_type=jnp.float32)  24.6 us
    dot_general x3, matrix products, per_device(): lax.dot_general(part_rows, pieces[:, goal], (((0,), (0,)), ((), ())), pre...  21.8 us
    dot_general x1, matrix products, per_device(): jnp.einsum('lrd,lfd->lrf', whole, enc_weight, preferred_element_type=jnp....  15.7 us
  transfers between devices with their start and end apart: 4, of which 4 were waited for; matrix products, arithmetic and copies ran while one was open for 0% of the time, Pallas kernels for 0%

commit v1 on v0

v1 whole, which is shorter than its diff:
```python
import functools

import jax
import jax.numpy as jnp
from jax import lax
from jax.experimental import pallas as pl
from jax.experimental.pallas import tpu as pltpu
from jax.sharding import PartitionSpec as P

BLOCK = 128
BAND = 0.2
LANES = 128
MESH = pl.DeviceIdType.MESH
MIB = 1 << 20


def bits(index, stages):
    return [(index // (1 << j)) % 2 for j in range(stages)]


def bases(index_bits, count):
    out = [0]
    for j, bit in enumerate(index_bits):
        out.append(out[-1] + bit * (count >> (j + 1)))
    return out


def partners(index, index_bits):
    return [index + (1 - 2 * bit) * (1 << j) for j, bit in enumerate(index_bits)]


def greet(n_feat, feat, mates):
    barrier = pltpu.get_barrier_semaphore()
    for mate in mates:
        pl.semaphore_signal(barrier, inc=1, device_id={"layer": mate}, device_id_type=MESH)

    def one(o, carry):
        pl.semaphore_signal(
            barrier, inc=1, device_id={"feat": (feat + o) % n_feat}, device_id_type=MESH
        )
        return carry

    lax.fori_loop(1, n_feat, one, 0)
    pl.semaphore_wait(barrier, len(mates) + n_feat - 1)


def remote(src, dst, send, recv, where):
    return pltpu.make_async_remote_copy(
        src_ref=src, dst_ref=dst, send_sem=send, recv_sem=recv, device_id=where, device_id_type=MESH
    )


def gather_kernel(n_feat, n_layer, x_ref, out_ref, z_send, z_recv, l_send, l_recv, own_sem):
    feat, place = lax.axis_index("feat"), lax.axis_index("layer")
    stages = n_layer.bit_length() - 1
    rows = x_ref.shape[1]
    width = x_ref.shape[2] // n_layer
    place_bits = bits(place, stages)
    base = bases(place_bits, n_layer)
    mates = partners(place, place_bits)
    greet(n_feat, feat, mates)

    def at(ref, source, first, count):
        return ref.at[
            :,
            pl.ds(pl.multiple_of(source * rows, rows), rows),
            pl.ds(pl.multiple_of(first * width, width), count * width),
        ]

    def z_copy(o):
        mine = at(out_ref, feat, base[stages], 1)
        src = x_ref.at[:, :, pl.ds(pl.multiple_of(base[stages] * width, width), width)]
        return remote(src, mine, z_send.at[o - 1], z_recv.at[o - 1], {"feat": (feat + o) % n_feat})

    def l_copy(j, o):
        part = at(out_ref, (feat + n_feat - o) % n_feat, base[j + 1], n_layer >> (j + 1))
        return remote(part, part, l_send.at[j, o - 1], l_recv.at[j, o - 1], {"layer": mates[j]})

    def start_z(o, carry):
        z_copy(o).start()
        return carry

    lax.fori_loop(1, n_feat, start_z, 0)
    own = pltpu.make_async_copy(
        x_ref, out_ref.at[:, pl.ds(pl.multiple_of(feat * rows, rows), rows), :], own_sem
    )
    own.start()
    for j in reversed(range(-1, stages)):

        def hop(o, carry, j=j):
            if j == stages - 1:
                z_copy(o).wait_recv()
            else:
                l_copy(j + 1, o).wait_recv()
            if j >= 0:
                l_copy(j, o).start()
            return carry

        lax.fori_loop(1, n_feat, hop, 0)

    def drain(o, carry):
        z_copy(o).wait_send()
        for j in range(stages):
            l_copy(j, o).wait_send()
        return carry

    lax.fori_loop(1, n_feat, drain, 0)
    own.wait()


def gather(inputs, n_feat, n_layer):
    layers, rows, width = inputs.shape
    stages = n_layer.bit_length() - 1
    return pl.pallas_call(
        functools.partial(gather_kernel, n_feat, n_layer),
        out_shape=jax.ShapeDtypeStruct((layers, rows * n_feat, width), inputs.dtype),
        in_specs=[pl.BlockSpec(memory_space=pltpu.VMEM)],
        out_specs=pl.BlockSpec(memory_space=pltpu.VMEM),
        scratch_shapes=[
            pltpu.SemaphoreType.DMA((n_feat - 1,)),
            pltpu.SemaphoreType.DMA((n_feat - 1,)),
            pltpu.SemaphoreType.DMA((stages, n_feat - 1)),
            pltpu.SemaphoreType.DMA((stages, n_feat - 1)),
            pltpu.SemaphoreType.DMA,
        ],
        compiler_params=pltpu.CompilerParams(
            collective_id=0, has_side_effects=True, vmem_limit_bytes=16 * MIB
        ),
        name="gather_rows",
    )(inputs)


def gate_tile(mask_ref, values):
    mask = mask_ref[0, 0]
    shape = (mask.shape[0], BLOCK, values.shape[1])
    return jnp.broadcast_to(mask[:, None, :], shape).reshape(values.shape)


def encode_kernel(x_ref, w_ref, bias_ref, thr_ref, mask_ref, pre_ref, turned_ref, hidden_ref):
    pre = (
        lax.dot_general(
            w_ref[0], x_ref[0], (((1,), (1,)), ((), ())), preferred_element_type=jnp.float32
        )
        + bias_ref[0]
    )
    squash = jax.nn.sigmoid((pre - thr_ref[0]) / BAND)
    hidden = (gate_tile(mask_ref, pre) * pre * squash).astype(jnp.bfloat16)
    pre_ref[0] = pre
    turned_ref[0] = hidden
    hidden_ref[0] = hidden.T


def encode(whole, enc_weight, bias, thr, mask):
    layers, count, width = whole.shape
    features = enc_weight.shape[1]
    tile = min(512, features)
    column = pl.BlockSpec((1, tile, 1), lambda l, t: (l, t, 0))
    turned = pl.BlockSpec((1, tile, count), lambda l, t: (l, t, 0))
    return pl.pallas_call(
        encode_kernel,
        grid=(layers, features // tile),
        out_shape=(
            jax.ShapeDtypeStruct((layers, features, count), jnp.float32),
            jax.ShapeDtypeStruct((layers, features, count), jnp.bfloat16),
            jax.ShapeDtypeStruct((layers, count, features), jnp.bfloat16),
        ),
        in_specs=[
            pl.BlockSpec((1, count, width), lambda l, t: (l, 0, 0)),
            pl.BlockSpec((1, tile, width), lambda l, t: (l, t, 0)),
            column,
            column,
            pl.BlockSpec((1, 1, tile // BLOCK, count), lambda l, t: (l, t, 0, 0)),
        ],
        out_specs=(turned, turned, pl.BlockSpec((1, count, tile), lambda l, t: (l, 0, t))),
        compiler_params=pltpu.CompilerParams(vmem_limit_bytes=40 * MIB),
        name="encode",
    )(whole, enc_weight, bias, thr, mask)


def exchange_kernel(
    n_feat, n_layer, hidden_ref, w_hbm, tgt_ref, err_ref, back_ref,
    wbuf, dec, z_got, w_sem, z_send, z_recv, g_send, g_recv, r_send, r_recv, a_send, a_recv, *got,
):
    feat, place = lax.axis_index("feat"), lax.axis_index("layer")
    stages = n_layer.bit_length() - 1
    layers, count, features = hidden_ref.shape
    rows = count // n_feat
    chunks = dec.shape[0]
    cols = n_layer * LANES
    splits = chunks // layers
    pairs = wbuf.shape[0]
    place_bits = bits(place, stages)
    base = bases(place_bits, n_layer)
    mates = partners(place, place_bits)
    mine = base[stages]
    held = [n_layer >> (j + 1) for j in range(stages)]

    def load(p, n):
        part = w_hbm.at[p, :, pl.ds(n * cols, cols)]
        return pltpu.make_async_copy(part, wbuf.at[p, n], w_sem.at[p, n])

    for n in range(splits):
        for p in range(pairs):
            load(p, n).start()
    greet(n_feat, feat, mates)

    tile = min(512, features)

    @pl.loop(0, layers * (features // tile))
    def _(i):
        l, t = i // (features // tile), i % (features // tile)
        back_ref[l, pl.ds(pl.multiple_of(t * tile, tile), tile), :] = jnp.zeros(
            (tile, count), jnp.float32
        )

    def reduce_copy(j, k):
        away = base[j] + (1 - place_bits[j]) * held[j]
        return remote(
            dec.at[k, pl.ds(away, held[j])], got[j].at[k],
            r_send.at[j, k], r_recv.at[j, k], {"layer": mates[j]},
        )

    def spread_copy(j, k):
        part = err_ref.at[k, pl.ds(base[j + 1], held[j])]
        return remote(part, part, a_send.at[j, k], a_recv.at[j, k], {"layer": mates[j]})

    def own_rows(which):
        return pl.ds(pl.multiple_of(which * rows, rows), rows)

    def all_bytes(k, sem):
        return pltpu.make_async_copy(z_got.at[k], z_got.at[k], sem)

    def decode(k):
        m, n = k % layers, k // layers
        wide = min(2, n_layer)

        def run(sources):
            for p in sources:
                load(p, n).wait()

            @pl.loop(0, n_layer // wide)
            def _(c):
                lanes = pl.ds(pl.multiple_of(c * wide * LANES, wide * LANES), wide * LANES)
                total = None
                for p, l in sources.items():
                    term = jnp.dot(
                        hidden_ref[l], wbuf[p, n, :, lanes], preferred_element_type=jnp.float32
                    )
                    total = term if total is None else total + term
                total = total.astype(jnp.bfloat16)
                for i in range(wide):
                    dec[k, c * wide + i] = total[:, i * LANES : (i + 1) * LANES]

        pl.when(m == 0)(lambda: run({0: 0}))
        pl.when(m == 1)(lambda: run({1: 0, 2: 1}))
        reduce_copy(0, k).start()

    def fold(j, k):
        reduce_copy(j, k).wait_recv()
        part = pl.ds(base[j + 1], held[j])
        total = dec[k, part].astype(jnp.float32) + got[j][k].astype(jnp.float32)
        dec[k, part] = total.astype(jnp.bfloat16)
        if j + 1 < stages:
            reduce_copy(j + 1, k).start()
        else:

            def send(o, carry):
                there = (feat + o) % n_feat
                remote(
                    dec.at[k, mine, own_rows(there)], z_got.at[k, o - 1],
                    z_send.at[k], z_recv.at[k], {"feat": there},
                ).start()
                return carry

            lax.fori_loop(1, n_feat, send, 0)

    def finish(k):
        all_bytes(k, z_recv.at[k]).wait()
        m, n = k % layers, k // layers
        total = dec[k, mine, own_rows(feat)].astype(jnp.float32)
        total = total + jnp.sum(z_got[k].astype(jnp.float32), axis=0)
        error = total - tgt_ref[m, n].astype(jnp.float32)
        part = err_ref.at[k, mine, own_rows(feat)]
        part[...] = error.astype(jnp.bfloat16)

        def send(o, carry):
            there = (feat + o) % n_feat
            remote(part, part, g_send.at[k], g_recv.at[k], {"feat": there}).start()
            return carry

        lax.fori_loop(1, n_feat, send, 0)

    def spread(j, k):
        if j == stages - 1:
            all_bytes(k, g_recv.at[k]).wait()
        else:
            spread_copy(j + 1, k).wait_recv()
        spread_copy(j, k).start()

    def pull(k):
        spread_copy(0, k).wait_recv()
        m, n = k % layers, k // layers

        def run(sources):
            error = jnp.concatenate([err_ref[k, b] for b in range(n_layer)], axis=1)
            for p, l in sources.items():

                @pl.loop(0, features // tile)
                def _(t, p=p, l=l):
                    part = pl.ds(pl.multiple_of(t * tile, tile), tile)
                    back_ref[l, part, :] += lax.dot_general(
                        wbuf[p, n, part, :], error, (((1,), (1,)), ((), ())),
                        preferred_element_type=jnp.float32,
                    )

        pl.when(m == 0)(lambda: run({0: 0}))
        pl.when(m == 1)(lambda: run({1: 0, 2: 1}))

    steps = [decode]
    steps += [functools.partial(fold, j) for j in range(stages)]
    steps += [finish]
    steps += [functools.partial(spread, j) for j in reversed(range(stages))]
    steps += [pull]

    @pl.loop(0, chunks + len(steps) - 1)
    def _(s):
        for late in reversed(range(1, len(steps) - 1)):
            k = s - late
            pl.when((k >= 0) & (k < chunks))(functools.partial(steps[late], k))
        pl.when(s < chunks)(functools.partial(decode, s))
        k = s - (len(steps) - 1)
        pl.when(k >= 0)(functools.partial(pull, k))

    @pl.loop(0, chunks)
    def _(k):
        all_bytes(k, z_send.at[k]).wait()
        all_bytes(k, g_send.at[k]).wait()
        for j in range(stages):
            reduce_copy(j, k).wait_send()
            spread_copy(j, k).wait_send()


def exchange(hidden, dec_weight, tgt, n_feat, n_layer):
    layers, count, features = hidden.shape
    pairs, _, width = dec_weight.shape
    stages = n_layer.bit_length() - 1
    splits = width // (n_layer * LANES)
    chunks = splits * layers
    rows = count // n_feat
    dma = pltpu.SemaphoreType.DMA
    vmem = pl.BlockSpec(memory_space=pltpu.VMEM)
    return pl.pallas_call(
        functools.partial(exchange_kernel, n_feat, n_layer),
        out_shape=(
            jax.ShapeDtypeStruct((chunks, n_layer, count, LANES), jnp.bfloat16),
            jax.ShapeDtypeStruct((layers, features, count), jnp.float32),
        ),
        in_specs=[vmem, pl.BlockSpec(memory_space=pl.ANY), vmem],
        out_specs=(vmem, vmem),
        scratch_shapes=[
            pltpu.VMEM((pairs, splits, features, n_layer * LANES), jnp.bfloat16),
            pltpu.VMEM((chunks, n_layer, count, LANES), jnp.bfloat16),
            pltpu.VMEM((chunks, n_feat - 1, rows, LANES), jnp.bfloat16),
            dma((pairs, splits)),
            dma((chunks,)),
            dma((chunks,)),
            dma((chunks,)),
            dma((chunks,)),
            dma((stages, chunks)),
            dma((stages, chunks)),
            dma((stages, chunks)),
            dma((stages, chunks)),
        ]
        + [
            pltpu.VMEM((chunks, n_layer >> (j + 1), count, LANES), jnp.bfloat16)
            for j in range(stages)
        ],
        compiler_params=pltpu.CompilerParams(
            collective_id=1, has_side_effects=True, vmem_limit_bytes=60 * MIB
        ),
        name="decode_exchange",
    )(hidden, dec_weight, tgt)


def grad_dec_kernel(layers, turned_ref, err_ref, out_ref):
    goal = (pl.program_id(0) + 1) // 2
    n_layer = err_ref.shape[1]
    cols = n_layer * LANES
    for n in range(err_ref.shape[0] // layers):
        error = jnp.concatenate([err_ref[n * layers + goal, b] for b in range(n_layer)], axis=1)
        out_ref[0, :, n * cols : (n + 1) * cols] = jnp.dot(
            turned_ref[0], error, preferred_element_type=jnp.float32
        ).astype(jnp.bfloat16)


def grad_dec(turned, err, pairs, width):
    layers, features, count = turned.shape
    tile = min(512, features)
    return pl.pallas_call(
        functools.partial(grad_dec_kernel, layers),
        grid=(pairs, features // tile),
        out_shape=jax.ShapeDtypeStruct((pairs, features, width), jnp.bfloat16),
        in_specs=[
            pl.BlockSpec((1, tile, count), lambda p, t: (p // 2, t, 0)),
            pl.BlockSpec(err.shape, lambda p, t: (0, 0, 0, 0)),
        ],
        out_specs=pl.BlockSpec((1, tile, width), lambda p, t: (p, t, 0)),
        compiler_params=pltpu.CompilerParams(vmem_limit_bytes=40 * MIB),
        name="grad_dec",
    )(turned, err)


def grad_enc_kernel(back_ref, pre_ref, thr_ref, mask_ref, x_ref, out_ref, bias_ref, gthr_ref):
    pre = pre_ref[0]
    back = back_ref[0]
    squash = jax.nn.sigmoid((pre - thr_ref[0]) / BAND)
    bend = squash * (1.0 - squash) / BAND
    gated = back * gate_tile(mask_ref, pre)
    curve = gated * pre * bend
    grad_pre = gated * squash + curve
    bias_ref[0] = jnp.sum(grad_pre, axis=1, keepdims=True)
    gthr_ref[0] = -jnp.sum(curve, axis=1, keepdims=True)
    out_ref[0] = jnp.dot(
        grad_pre.astype(jnp.bfloat16), x_ref[0], preferred_element_type=jnp.float32
    ).astype(jnp.bfloat16)


def grad_enc(back, pre, thr, mask, whole):
    layers, features, count = pre.shape
    width = whole.shape[2]
    tile = min(512, features)
    column = pl.BlockSpec((1, tile, 1), lambda l, t: (l, t, 0))
    turned = pl.BlockSpec((1, tile, count), lambda l, t: (l, t, 0))
    return pl.pallas_call(
        grad_enc_kernel,
        grid=(layers, features // tile),
        out_shape=(
            jax.ShapeDtypeStruct((layers, features, width), jnp.bfloat16),
            jax.ShapeDtypeStruct((layers, features, 1), jnp.float32),
            jax.ShapeDtypeStruct((layers, features, 1), jnp.float32),
        ),
        in_specs=[
            turned,
            turned,
            column,
            pl.BlockSpec((1, 1, tile // BLOCK, count), lambda l, t: (l, t, 0, 0)),
            pl.BlockSpec((1, count, width), lambda l, t: (l, 0, 0)),
        ],
        out_specs=(pl.BlockSpec((1, tile, width), lambda l, t: (l, t, 0)), column, column),
        compiler_params=pltpu.CompilerParams(vmem_limit_bytes=40 * MIB),
        name="grad_enc",
    )(back, pre, thr, mask, whole)


def per_device(n_feat, n_layer, inputs, targets, block_mask, enc_weight, enc_bias, threshold, dec_weight):
    layers, features, width = enc_weight.shape
    place = lax.axis_index("layer")
    rows = inputs.shape[1]
    count = block_mask.shape[2]
    tile = min(512, features)
    blocks = features // BLOCK
    mask = lax.dynamic_slice_in_dim(block_mask, place * blocks, blocks, 1).astype(jnp.float32)
    mask = mask.reshape(layers, features // tile, tile // BLOCK, count)
    bias, thr = enc_bias[:, :, None], threshold[:, :, None]
    stages = n_layer.bit_length() - 1
    mine = bases(bits(place, stages), n_layer)[stages]
    tgt = targets.reshape(rows, layers, width // (n_layer * LANES), n_layer, LANES)
    tgt = lax.dynamic_index_in_dim(tgt, mine, 3, keepdims=False).transpose(1, 2, 0, 3)

    whole = gather(inputs, n_feat, n_layer)
    pre, turned, hidden = encode(whole, enc_weight, bias, thr, mask)
    err, back = exchange(hidden, dec_weight, tgt, n_feat, n_layer)
    dec_grads = grad_dec(turned, err, dec_weight.shape[0], width)
    enc_grads, grad_bias, grad_thr = grad_enc(back, pre, thr, mask, whole)
    return (
        enc_grads,
        grad_bias.reshape(layers, features),
        grad_thr.reshape(layers, features),
        dec_grads,
    )


def solution(mesh):
    return jax.shard_map(
        functools.partial(per_device, mesh.shape["feat"], mesh.shape["layer"]),
        mesh=mesh,
        in_specs=(
            P(None, ("groups", "feat"), None),
            P(("groups", "feat"), None, None),
            P(None, "feat", "groups"),
            P(None, ("feat", "layer"), None),
            P(None, ("feat", "layer")),
            P(None, ("feat", "layer")),
            P(None, ("feat", "layer"), None),
        ),
        out_specs=(
            P("groups", ("feat", "layer"), None),
            P("groups", ("feat", "layer")),
            P("groups", ("feat", "layer")),
            P("groups", ("feat", "layer"), None),
        ),
        check_vma=False,
    )
```

time: 451 us -> 210 us (0.47); the launches traced: 443 us -> 209 us
  waiting for transfers between devices: 281 us -> 0 us
  Pallas kernels: 0 us -> 181 us
  matrix products: 116 us -> 0 us
  other arithmetic: 30.1 us -> 6.58 us
  local copies, waits for them, and re-layouts: 0.05 us -> 20.9 us
  between operations: 14.3 us -> 0.77 us
    pallas_call x0 -> x5, Pallas kernels: none -> 181 us  [the longest x1 90.6 us: exchange(): pl.pallas_call(functools.partial(exchange_kernel, n_feat, n_layer), out_s...]
    all_gather x2 -> x0, waiting for transfers between devices: 166 us -> none  [the longest x1 85.1 us: per_device(): whole = lax.all_gather(inputs, 'feat', axis=1, tiled=True)]
    dot_general x12 -> x0, matrix products: 116 us -> none  [the longest x3 32.1 us: per_device(): lax.dot_general(pieces[:, goal], dec_weight[index], (((1,), (1,)), ((), (...]
    reduce_scatter x1 -> x0, waiting for transfers between devices: 75.4 us -> none  [per_device(): lax.psum_scatter(jnp.stack(columns, 1).astype(jnp.bfloat16), 'feat', scat...]
    psum x1 -> x0, waiting for transfers between devices: 38.9 us -> none  [per_device(): own_sum = lax.psum(decoded, 'layer').astype(jnp.float32)]
    another operation x2 -> x0, other arithmetic: 16.8 us -> none  [the longest x1 14.5 us: per_device(): dec_sum, back_grad = (jnp.stack(new_grads, 0), back_grad)]
    unnamed x24 -> x25, local copies, waits for them, and re-layouts: 0.05 us -> 15.9 us
    reduce_sum x1 -> x0, other arithmetic: 9.85 us -> none  [per_device(): grad_bias = jnp.sum(grad_pre, axis=1)]
  transfers between devices with their start and end apart: 4 -> 0, of which waited for: 4 -> 0; matrix products, arithmetic and copies ran while one was open for 0% -> 0% of each run, Pallas kernels for 0% -> 0%
where the time goes in v1:
time: 210 us; the launch traced here: 209 us
  Pallas kernels  181 us (86%)
  local copies, waits for them, and re-layouts  20.9 us (10%)
  other arithmetic  6.58 us (3%)
    pallas_call x1, Pallas kernels, exchange(): pl.pallas_call(functools.partial(exchange_kernel, n_feat, n_layer), out_s...  90.6 us
    pallas_call x1, Pallas kernels, gather(): pl.pallas_call(functools.partial(gather_kernel, n_feat, n_layer), out_sha...  37.8 us
    pallas_call x1, Pallas kernels, grad_enc(): pl.pallas_call(grad_enc_kernel, grid=(layers, features // tile), out_shap...  18.7 us
    pallas_call x1, Pallas kernels, encode(): pl.pallas_call(encode_kernel, grid=(layers, features // tile), out_shape=...  17.1 us
    pallas_call x1, Pallas kernels, grad_dec(): pl.pallas_call(functools.partial(grad_dec_kernel, layers), grid=(pairs, f...  16.7 us
    unnamed x25, local copies, waits for them, and re-layouts  15.9 us
    pallas_call x2, other arithmetic, grad_enc(): pl.pallas_call(grad_enc_kernel, grid=(layers, features // tile), out_shap...  5.64 us

profile of v1, /device:TPU:0, one launch (start us, length us, event | category | flops | bytes accessed | tf_op | source)
XLA Modules:
  0.0 209.2 jit_solution(17271225316424266628)
XLA Ops:
  0.6 0.0 copy-start.10
  0.6 0.0 copy-start.11
  0.7 0.0 copy-start.9
  0.7 0.9 dynamic-slice_convert_fusion
  1.7 1.7 reshape.21
  3.4 0.5 constant_dynamic-slice_fusion
  4.0 0.8 copy.18
  4.8 0.0 copy-done.10
  4.8 0.6 copy.13.thr_ref
  5.4 0.0 copy-done.11
  5.4 2.0 copy.12.bias_ref
  7.4 0.0 copy-done.9
  7.4 0.0 copy-start.2
  7.4 37.8 %gather_rows.1.x_ref = bf16[2,512,2048]{2,1,0:T(8,128)(2,1)S(1)} custom-call(bf16[2,128,2048]{2,1,0:T(8,128)(2,1)S(1)} %copy-done.9), custom_call_target="tpu_custom_call" | custom-call | tf_op jit(solution)/shard_map/gather_rows/pallas_call | solution.py:114
  45.2 0.0 copy-start
  45.2 2.0 copy-done
  47.2 0.0 copy-done.2
  47.2 17.1 %encode.1 = (f32[2,2048,512]{2,1,0:T(8,128)}, bf16[2,2048,512]{2,1,0:T(8,128)(2,1)S(1)}, bf16[2,512,2048]{2,1,0:T(8,128)(2,1)S(1)}) custom-call(bf16[2,512,2048]{2,1,0:T(8,128)(2,1)} %copy-done, bf16[2,2048,2048]{2,1,0:T(8,128)(2,1)} %w_ref.1, f32[2,2048,1]{2,1,0:T(8,128)S(1)} %copy-done.2, f32[2,2048,1]{2,1,0:T(8,128)S(1)} %copy.13.thr_ref, ...), custom_call_target="tpu_custom_call" | custom-call | tf_op jit(solution)/shard_map/encode/pallas_call | solution.py:159
  64.4 0.0 copy-start.3
  64.4 1.9 copy-done.3
  66.3 0.0 copy-start.4
  66.3 2.0 copy-done.4
  68.3 90.6 %decode_exchange.1 = (bf16[8,4,512,128]{3,2,1,0:T(8,128)(2,1)}, f32[2,2048,512]{2,1,0:T(8,128)}) custom-call(bf16[2,512,2048]{2,1,0:T(8,128)(2,1)} %copy-done.3, bf16[3,2048,2048]{2,1,0:T(8,128)(2,1)} %w_hbm.1, bf16[2,4,128,128]{3,2,1,0:T(8,128)(2,1)} %bitcast.7), custom_call_target="tpu_custom_call" | custom-call | tf_op jit(solution)/shard_map/decode_exchange/pallas_call | solution.py:352
  158.9 0.0 copy-start.1
  158.9 2.2 %copy-done.1 = bf16[2,512,2048]{2,1,0:T(8,128)(2,1)S(1)} copy-done((bf16[2,512,2048]{2,1,0:T(8,128)(2,1)S(1)}, bf16[2,512,2048]{2,1,0:T(8,128)(2,1)}, u32[]{:S(2)}) %copy-start.1) | copy-done | bytes 4194328
  161.0 18.7 %grad_enc.1 = (bf16[2,2048,2048]{2,1,0:T(8,128)(2,1)}, f32[2,2048,1]{2,1,0:T(8,128)S(1)}, f32[2,2048,1]{2,1,0:T(8,128)S(1)}) custom-call(f32[2,2048,512]{2,1,0:T(8,128)} %get-tuple-element.13.back_ref, f32[2,2048,512]{2,1,0:T(8,128)} %get-tuple-element.14.pre_ref, f32[2,2048,1]{2,1,0:T(8,128)S(1)} %copy.13.thr_ref, f32[2,4,4,512]{3,2,1,0:T(4,128)S(1)} %reshape.20.mask_ref, ...), custom_call_target="tpu_custom_call" | custom-call | tf_op jit(solution)/shard_map/grad_enc/pallas_call | solution.py:434
  179.8 0.0 copy-start.7
  179.8 1.3 copy-done.7
  181.1 0.0 copy-start.8
  181.1 1.3 copy-done.8
  182.4 2.8 %reduce = f32[2,2048]{1,0:T(2,128)} reduce(f32[2,2048,1]{2,1,0:T(8,128)} %copy-done.8, f32[]{:T(128)} %constant.51), dimensions={2}, to_apply=%get-tuple-element.16.reduce_sub_computation | reduce | bytes 32772 | tf_op jit(solution)/shard_map/grad_enc/pallas_call | solution.py:434
  185.2 2.8 %reduce.1 = f32[2,2048]{1,0:T(2,128)} reduce(f32[2,2048,1]{2,1,0:T(8,128)} %copy-done.7, f32[]{:T(128)} %constant.51), dimensions={2}, to_apply=%get-tuple-element.17.reduce_sub_computation | reduce | bytes 32772 | tf_op jit(solution)/shard_map/grad_enc/pallas_call | solution.py:434
  188.1 0.0 copy-start.5
  188.1 2.2 %copy-done.5 = bf16[2,2048,512]{2,1,0:T(8,128)(2,1)S(1)} copy-done((bf16[2,2048,512]{2,1,0:T(8,128)(2,1)S(1)}, bf16[2,2048,512]{2,1,0:T(8,128)(2,1)}, u32[]{:S(2)}) %copy-start.5) | copy-done | bytes 4194328
  190.3 0.0 copy-start.6
  190.3 2.2 %copy-done.6 = bf16[8,4,512,128]{3,2,1,0:T(8,128)(2,1)S(1)} copy-done((bf16[8,4,512,128]{3,2,1,0:T(8,128)(2,1)S(1)}, bf16[8,4,512,128]{3,2,1,0:T(8,128)(2,1)}, u32[]{:S(2)}) %copy-start.6) | copy-done | bytes 4194328
  192.4 16.7 %grad_dec.1 = bf16[3,2048,2048]{2,1,0:T(8,128)(2,1)} custom-call(bf16[2,2048,512]{2,1,0:T(8,128)(2,1)S(1)} %copy-done.5, bf16[8,4,512,128]{3,2,1,0:T(8,128)(2,1)S(1)} %copy-done.6), custom_call_target="tpu_custom_call" | custom-call | tf_op jit(solution)/shard_map/grad_dec/pallas_call | solution.py:399
  (1 shorter events, 0.0 us)
Async XLA Ops:
  0.6 4.1 %copy-start.10 = (f32[2,2048]{1,0:T(2,128)S(1)}, f32[2,2048]{1,0:T(2,128)}, u32[]{:S(2)}) copy-start(f32[2,2048]{1,0:T(2,128)} %param.12) | copy-start | bytes 49156
  0.6 4.8 %copy-start.11 = (f32[2,2048]{1,0:T(2,128)S(1)}, f32[2,2048]{1,0:T(2,128)}, u32[]{:S(2)}) copy-start(f32[2,2048]{1,0:T(2,128)} %param.11) | copy-start | bytes 49156
  0.7 6.7 %copy-start.9 = (bf16[2,128,2048]{2,1,0:T(8,128)(2,1)S(1)}, bf16[2,128,2048]{2,1,0:T(8,128)(2,1)}, u32[]{:S(2)}) copy-start(bf16[2,128,2048]{2,1,0:T(8,128)(2,1)} %x_ref.1) | copy-start | bytes 3145732
  7.4 39.8 %copy-start.2 = (f32[2,2048,1]{2,1,0:T(8,128)S(1)}, f32[2,2048,1]{2,1,0:T(8,128)}, u32[]{:S(2)}) copy-start(f32[2,2048,1]{2,1,0:T(8,128)} %copy.12.bias_ref) | copy-start | bytes 49156
  45.2 2.0 copy-start
  64.4 1.9 copy-start.3
  66.3 2.0 copy-start.4
  158.9 2.2 %copy-start.1 = (bf16[2,512,2048]{2,1,0:T(8,128)(2,1)S(1)}, bf16[2,512,2048]{2,1,0:T(8,128)(2,1)}, u32[]{:S(2)}) copy-start(bf16[2,512,2048]{2,1,0:T(8,128)(2,1)} %copy-done) | copy-start | bytes 12582916
  179.8 1.3 copy-start.7
  181.1 1.3 copy-start.8
  188.1 2.2 %copy-start.5 = (bf16[2,2048,512]{2,1,0:T(8,128)(2,1)S(1)}, bf16[2,2048,512]{2,1,0:T(8,128)(2,1)}, u32[]{:S(2)}) copy-start(bf16[2,2048,512]{2,1,0:T(8,128)(2,1)} %copy-done.4) | copy-start | bytes 12582916
  190.3 2.2 %copy-start.6 = (bf16[8,4,512,128]{3,2,1,0:T(8,128)(2,1)S(1)}, bf16[8,4,512,128]{3,2,1,0:T(8,128)(2,1)}, u32[]{:S(2)}) copy-start(bf16[8,4,512,128]{3,2,1,0:T(8,128)(2,1)} %get-tuple-element.19.err_ref) | copy-start | bytes 12582916

commit v2 on v1

--- a/solution.py
+++ b/solution.py
@@ -60,27 +60,32 @@
     mates = partners(place, place_bits)
     greet(n_feat, feat, mates)
 
-    def at(ref, source, first, count):
+    layers = x_ref.shape[0]
+    pieces = (n_feat - 1) * layers
+
+    def at(ref, l, source, first, count):
         return ref.at[
-            :,
+            l,
             pl.ds(pl.multiple_of(source * rows, rows), rows),
             pl.ds(pl.multiple_of(first * width, width), count * width),
         ]
 
-    def z_copy(o):
-        mine = at(out_ref, feat, base[stages], 1)
-        src = x_ref.at[:, :, pl.ds(pl.multiple_of(base[stages] * width, width), width)]
-        return remote(src, mine, z_send.at[o - 1], z_recv.at[o - 1], {"feat": (feat + o) % n_feat})
-
-    def l_copy(j, o):
-        part = at(out_ref, (feat + n_feat - o) % n_feat, base[j + 1], n_layer >> (j + 1))
-        return remote(part, part, l_send.at[j, o - 1], l_recv.at[j, o - 1], {"layer": mates[j]})
+    def z_copy(i):
+        o, l = i // layers + 1, i % layers
+        mine = at(out_ref, l, feat, base[stages], 1)
+        src = x_ref.at[l, :, pl.ds(pl.multiple_of(base[stages] * width, width), width)]
+        return remote(src, mine, z_send.at[i], z_recv.at[i], {"feat": (feat + o) % n_feat})
+
+    def l_copy(j, i):
+        o, l = i // layers + 1, i % layers
+        part = at(out_ref, l, (feat + n_feat - o) % n_feat, base[j + 1], n_layer >> (j + 1))
+        return remote(part, part, l_send.at[j, i], l_recv.at[j, i], {"layer": mates[j]})
 
     def start_z(o, carry):
         z_copy(o).start()
         return carry
 
-    lax.fori_loop(1, n_feat, start_z, 0)
+    lax.fori_loop(0, pieces, start_z, 0)
     own = pltpu.make_async_copy(
         x_ref, out_ref.at[:, pl.ds(pl.multiple_of(feat * rows, rows), rows), :], own_sem
     )
@@ -96,7 +101,7 @@
                 l_copy(j, o).start()
             return carry
 
-        lax.fori_loop(1, n_feat, hop, 0)
+        lax.fori_loop(0, pieces, hop, 0)
 
     def drain(o, carry):
         z_copy(o).wait_send()
@@ -104,7 +109,7 @@
             l_copy(j, o).wait_send()
         return carry
 
-    lax.fori_loop(1, n_feat, drain, 0)
+    lax.fori_loop(0, pieces, drain, 0)
     own.wait()
 
 
@@ -117,34 +122,46 @@
         in_specs=[pl.BlockSpec(memory_space=pltpu.VMEM)],
         out_specs=pl.BlockSpec(memory_space=pltpu.VMEM),
         scratch_shapes=[
-            pltpu.SemaphoreType.DMA((n_feat - 1,)),
-            pltpu.SemaphoreType.DMA((n_feat - 1,)),
-            pltpu.SemaphoreType.DMA((stages, n_feat - 1)),
-            pltpu.SemaphoreType.DMA((stages, n_feat - 1)),
+            pltpu.SemaphoreType.DMA(((n_feat - 1) * layers,)),
+            pltpu.SemaphoreType.DMA(((n_feat - 1) * layers,)),
+            pltpu.SemaphoreType.DMA((stages, (n_feat - 1) * layers)),
+            pltpu.SemaphoreType.DMA((stages, (n_feat - 1) * layers)),
             pltpu.SemaphoreType.DMA,
         ],
         compiler_params=pltpu.CompilerParams(
-            collective_id=0, has_side_effects=True, vmem_limit_bytes=16 * MIB
+            collective_id=0, has_side_effects=True, vmem_limit_bytes=60 * MIB
         ),
         name="gather_rows",
     )(inputs)
 
 
-def gate_tile(mask_ref, values):
-    mask = mask_ref[0, 0]
+def column_of(ref, l, t, tile):
+    row = ref[pl.ds(l, 1), pl.ds(pl.multiple_of(t * tile, tile), tile)]
+    return jnp.broadcast_to(row, (LANES, tile)).T[:, :1]
+
+
+def squash_of(pre, thr):
+    return 0.5 + 0.5 * jnp.tanh((pre - thr) * (0.5 / BAND))
+
+
+def row_of(column):
+    return jnp.broadcast_to(column, (column.shape[0], LANES)).T[:1]
+
+
+def gate_tile(mask_ref, l, t, values):
+    mask = mask_ref[l, t]
     shape = (mask.shape[0], BLOCK, values.shape[1])
     return jnp.broadcast_to(mask[:, None, :], shape).reshape(values.shape)
 
 
 def encode_kernel(x_ref, w_ref, bias_ref, thr_ref, mask_ref, pre_ref, turned_ref, hidden_ref):
-    pre = (
-        lax.dot_general(
-            w_ref[0], x_ref[0], (((1,), (1,)), ((), ())), preferred_element_type=jnp.float32
-        )
-        + bias_ref[0]
-    )
-    squash = jax.nn.sigmoid((pre - thr_ref[0]) / BAND)
-    hidden = (gate_tile(mask_ref, pre) * pre * squash).astype(jnp.bfloat16)
+    l, t = pl.program_id(0), pl.program_id(1)
+    tile = w_ref.shape[1]
+    pre = lax.dot_general(
+        w_ref[0], x_ref[0], (((1,), (1,)), ((), ())), preferred_element_type=jnp.float32
+    ) + column_of(bias_ref, l, t, tile)
+    squash = squash_of(pre, column_of(thr_ref, l, t, tile))
+    hidden = (gate_tile(mask_ref, l, t, pre) * pre * squash).astype(jnp.bfloat16)
     pre_ref[0] = pre
     turned_ref[0] = hidden
     hidden_ref[0] = hidden.T
@@ -153,8 +170,8 @@
 def encode(whole, enc_weight, bias, thr, mask):
     layers, count, width = whole.shape
     features = enc_weight.shape[1]
-    tile = min(512, features)
-    column = pl.BlockSpec((1, tile, 1), lambda l, t: (l, t, 0))
+    tile = min(1024, features)
+    row = pl.BlockSpec((layers, features), lambda l, t: (0, 0))
     turned = pl.BlockSpec((1, tile, count), lambda l, t: (l, t, 0))
     return pl.pallas_call(
         encode_kernel,
@@ -167,12 +184,12 @@
         in_specs=[
             pl.BlockSpec((1, count, width), lambda l, t: (l, 0, 0)),
             pl.BlockSpec((1, tile, width), lambda l, t: (l, t, 0)),
-            column,
-            column,
-            pl.BlockSpec((1, 1, tile // BLOCK, count), lambda l, t: (l, t, 0, 0)),
+            row,
+            row,
+            pl.BlockSpec(mask.shape, lambda l, t: (0, 0, 0, 0)),
         ],
         out_specs=(turned, turned, pl.BlockSpec((1, count, tile), lambda l, t: (l, 0, t))),
-        compiler_params=pltpu.CompilerParams(vmem_limit_bytes=40 * MIB),
+        compiler_params=pltpu.CompilerParams(vmem_limit_bytes=60 * MIB),
         name="encode",
     )(whole, enc_weight, bias, thr, mask)
 
@@ -395,7 +412,7 @@
 
 def grad_dec(turned, err, pairs, width):
     layers, features, count = turned.shape
-    tile = min(512, features)
+    tile = min(1024, features)
     return pl.pallas_call(
         functools.partial(grad_dec_kernel, layers),
         grid=(pairs, features // tile),
@@ -405,21 +422,24 @@
             pl.BlockSpec(err.shape, lambda p, t: (0, 0, 0, 0)),
         ],
         out_specs=pl.BlockSpec((1, tile, width), lambda p, t: (p, t, 0)),
-        compiler_params=pltpu.CompilerParams(vmem_limit_bytes=40 * MIB),
+        compiler_params=pltpu.CompilerParams(vmem_limit_bytes=60 * MIB),
         name="grad_dec",
     )(turned, err)
 
 
 def grad_enc_kernel(back_ref, pre_ref, thr_ref, mask_ref, x_ref, out_ref, bias_ref, gthr_ref):
+    l, t = pl.program_id(0), pl.program_id(1)
     pre = pre_ref[0]
     back = back_ref[0]
-    squash = jax.nn.sigmoid((pre - thr_ref[0]) / BAND)
-    bend = squash * (1.0 - squash) / BAND
-    gated = back * gate_tile(mask_ref, pre)
+    tile = pre.shape[0]
+    squash = squash_of(pre, column_of(thr_ref, l, t, tile))
+    bend = squash * (1.0 - squash) * (1.0 / BAND)
+    gated = back * gate_tile(mask_ref, l, t, pre)
     curve = gated * pre * bend
     grad_pre = gated * squash + curve
-    bias_ref[0] = jnp.sum(grad_pre, axis=1, keepdims=True)
-    gthr_ref[0] = -jnp.sum(curve, axis=1, keepdims=True)
+    place = (pl.ds(l, 1), pl.ds(pl.multiple_of(t * tile, tile), tile))
+    bias_ref[place] = row_of(jnp.sum(grad_pre, axis=1, keepdims=True))
+    gthr_ref[place] = row_of(-jnp.sum(curve, axis=1, keepdims=True))
     out_ref[0] = jnp.dot(
         grad_pre.astype(jnp.bfloat16), x_ref[0], preferred_element_type=jnp.float32
     ).astype(jnp.bfloat16)
@@ -428,26 +448,26 @@
 def grad_enc(back, pre, thr, mask, whole):
     layers, features, count = pre.shape
     width = whole.shape[2]
-    tile = min(512, features)
-    column = pl.BlockSpec((1, tile, 1), lambda l, t: (l, t, 0))
+    tile = min(1024, features)
+    row = pl.BlockSpec((layers, features), lambda l, t: (0, 0))
     turned = pl.BlockSpec((1, tile, count), lambda l, t: (l, t, 0))
     return pl.pallas_call(
         grad_enc_kernel,
         grid=(layers, features // tile),
         out_shape=(
             jax.ShapeDtypeStruct((layers, features, width), jnp.bfloat16),
-            jax.ShapeDtypeStruct((layers, features, 1), jnp.float32),
-            jax.ShapeDtypeStruct((layers, features, 1), jnp.float32),
+            jax.ShapeDtypeStruct((layers, features), jnp.float32),
+            jax.ShapeDtypeStruct((layers, features), jnp.float32),
         ),
         in_specs=[
             turned,
             turned,
-            column,
-            pl.BlockSpec((1, 1, tile // BLOCK, count), lambda l, t: (l, t, 0, 0)),
+            row,
+            pl.BlockSpec(mask.shape, lambda l, t: (0, 0, 0, 0)),
             pl.BlockSpec((1, count, width), lambda l, t: (l, 0, 0)),
         ],
-        out_specs=(pl.BlockSpec((1, tile, width), lambda l, t: (l, t, 0)), column, column),
-        compiler_params=pltpu.CompilerParams(vmem_limit_bytes=40 * MIB),
+        out_specs=(pl.BlockSpec((1, tile, width), lambda l, t: (l, t, 0)), row, row),
+        compiler_params=pltpu.CompilerParams(vmem_limit_bytes=60 * MIB),
         name="grad_enc",
     )(back, pre, thr, mask, whole)
 
@@ -457,27 +477,21 @@
     place = lax.axis_index("layer")
     rows = inputs.shape[1]
     count = block_mask.shape[2]
-    tile = min(512, features)
+    tile = min(1024, features)
     blocks = features // BLOCK
     mask = lax.dynamic_slice_in_dim(block_mask, place * blocks, blocks, 1).astype(jnp.float32)
     mask = mask.reshape(layers, features // tile, tile // BLOCK, count)
-    bias, thr = enc_bias[:, :, None], threshold[:, :, None]
     stages = n_layer.bit_length() - 1
     mine = bases(bits(place, stages), n_layer)[stages]
     tgt = targets.reshape(rows, layers, width // (n_layer * LANES), n_layer, LANES)
     tgt = lax.dynamic_index_in_dim(tgt, mine, 3, keepdims=False).transpose(1, 2, 0, 3)
 
     whole = gather(inputs, n_feat, n_layer)
-    pre, turned, hidden = encode(whole, enc_weight, bias, thr, mask)
+    pre, turned, hidden = encode(whole, enc_weight, enc_bias, threshold, mask)
     err, back = exchange(hidden, dec_weight, tgt, n_feat, n_layer)
     dec_grads = grad_dec(turned, err, dec_weight.shape[0], width)
-    enc_grads, grad_bias, grad_thr = grad_enc(back, pre, thr, mask, whole)
-    return (
-        enc_grads,
-        grad_bias.reshape(layers, features),
-        grad_thr.reshape(layers, features),
-        dec_grads,
-    )
+    enc_grads, grad_bias, grad_thr = grad_enc(back, pre, threshold, mask, whole)
+    return enc_grads, grad_bias, grad_thr, dec_grads
 
 
 def solution(mesh):

time: 210 us -> 192 us (0.914)
  local copies, waits for them, and re-layouts: 20.9 us -> 3.08 us
  Pallas kernels: 181 us -> 187 us
  other arithmetic: 6.58 us -> 1.49 us
    unnamed x25 -> x1, local copies, waits for them, and re-layouts: 15.9 us -> 0.8 us
    pallas_call x2 -> x0, other arithmetic: 5.64 us -> none  [grad_enc(): pl.pallas_call(grad_enc_kernel, grid=(layers, features // tile), out_shap...]
    broadcast_in_dim x2 -> x0, local copies, waits for them, and re-layouts: 2.6 us -> none  [per_device(): bias, thr = (enc_bias[:, :, None], threshold[:, :, None])]
where the time goes in v2:
time: 192 us
  Pallas kernels  187 us (97%)
  local copies, waits for them, and re-layouts  3.08 us (2%)
    pallas_call x1, Pallas kernels, exchange(): pl.pallas_call(functools.partial(exchange_kernel, n_feat, n_layer), out_s...  91.6 us
    pallas_call x1, Pallas kernels, gather(): pl.pallas_call(functools.partial(gather_kernel, n_feat, n_layer), out_sha...  38.1 us
    pallas_call x1, Pallas kernels, grad_enc(): pl.pallas_call(grad_enc_kernel, grid=(layers, features // tile), out_shap...  19.7 us
    pallas_call x1, Pallas kernels, encode(): pl.pallas_call(encode_kernel, grid=(layers, features // tile), out_shape=...  18.8 us
    pallas_call x1, Pallas kernels, grad_dec(): pl.pallas_call(functools.partial(grad_dec_kernel, layers), grid=(pairs, f...  18.8 us

profile of v2, /device:TPU:0, one launch (start us, length us, event | category | flops | bytes accessed | tf_op | source)
XLA Modules:
  0.0 192.3 jit_solution(13184678130107480075)
XLA Ops:
  0.7 1.5 convert_bitcast_fusion.mask_ref
  2.2 1.7 reshape.15
  3.9 0.5 constant_dynamic-slice_fusion
  4.5 0.8 copy.14
  5.3 38.1 %gather_rows.1.x_ref = bf16[2,512,2048]{2,1,0:T(8,128)(2,1)} custom-call(bf16[2,128,2048]{2,1,0:T(8,128)(2,1)} %x_ref.1), custom_call_target="tpu_custom_call" | custom-call | tf_op jit(solution)/shard_map/gather_rows/pallas_call | solution.py:119
  43.4 18.8 %encode.1 = (f32[2,2048,512]{2,1,0:T(8,128)}, bf16[2,2048,512]{2,1,0:T(8,128)(2,1)}, bf16[2,512,2048]{2,1,0:T(8,128)(2,1)}) custom-call(bf16[2,512,2048]{2,1,0:T(8,128)(2,1)} %gather_rows.1.x_ref, bf16[2,2048,2048]{2,1,0:T(8,128)(2,1)} %w_ref.1, f32[2,2048]{1,0:T(2,128)} %bias_ref.1, f32[2,2048]{1,0:T(2,128)} %thr_ref.3, ...), custom_call_target="tpu_custom_call" | custom-call | tf_op jit(solution)/shard_map/encode/pallas_call | solution.py:176
  62.2 91.6 %decode_exchange.1 = (bf16[8,4,512,128]{3,2,1,0:T(8,128)(2,1)}, f32[2,2048,512]{2,1,0:T(8,128)}) custom-call(bf16[2,512,2048]{2,1,0:T(8,128)(2,1)} %get-tuple-element.12.hidden_ref, bf16[3,2048,2048]{2,1,0:T(8,128)(2,1)} %w_hbm.1, bf16[2,4,128,128]{3,2,1,0:T(8,128)(2,1)} %bitcast.7), custom_call_target="tpu_custom_call" | custom-call | tf_op jit(solution)/shard_map/decode_exchange/pallas_call | solution.py:369
  153.8 19.7 %grad_enc.1 = (bf16[2,2048,2048]{2,1,0:T(8,128)(2,1)}, f32[2,2048]{1,0:T(2,128)}, f32[2,2048]{1,0:T(2,128)}) custom-call(f32[2,2048,512]{2,1,0:T(8,128)} %get-tuple-element.13.back_ref, f32[2,2048,512]{2,1,0:T(8,128)} %get-tuple-element.14.pre_ref, f32[2,2048]{1,0:T(2,128)} %thr_ref.3, f32[2,2,8,512]{3,2,1,0:T(8,128)} %convert_bitcast_fusion.mask_ref, ...), custom_call_target="tpu_custom_call" | custom-call | tf_op jit(solution)/shard_map/grad_enc/pallas_call | solution.py:454
  173.5 18.8 %grad_dec.1 = bf16[3,2048,2048]{2,1,0:T(8,128)(2,1)} custom-call(bf16[2,2048,512]{2,1,0:T(8,128)(2,1)} %get-tuple-element.18.turned_ref, bf16[8,4,512,128]{3,2,1,0:T(8,128)(2,1)} %get-tuple-element.19.err_ref), custom_call_target="tpu_custom_call" | custom-call | tf_op jit(solution)/shard_map/grad_dec/pallas_call | solution.py:416
